TPU v7x, 256 devices: a whole 4x4x8 slice. The times are simulated.
256 devices in a mesh: slab: 32 (over y, z_lo, core), chan: 8 (over z_hi, x).
Axes of the slice: x: 4, y: 4, z: 8 (z_hi: 2, z_lo: 4; z = z_hi * 4 + z_lo), core: 2. Of those that a mesh axis runs over, the one named last changes fastest.
Arguments:
- iterate: bfloat16 [24576, 4096], P('chan', 'slab'), may hold values from -6 to 6
- source: bfloat16 [24576, 4096], P('chan', 'slab'), may hold values from -6 to 6
- coupling: bfloat16 [192, 12, 128, 128], P('chan'), may hold values from -0.15625 to 0.15625
- pair_rows: int32 [192, 12], P('chan'), may hold values from 0 to 191, all different within a row
- diag_pot: float32 [24576, 512], P('chan', 'slab'), may hold values from -2 to 2
- profile: float32 [512], P('slab'), may hold values from 0.3 to 3
- regular: float32 [24576, 512], P('chan', 'slab'), may hold values from -6 to 6
- irregular: float32 [24576, 512], P('chan', 'slab'), may hold values from -6 to 6
Outputs:
- updated: bfloat16 [24576, 4096], P('chan', 'slab')
Inputs may be any that keep to these rules, and one draw needn't show every extreme that they name: `pair_rows`: each column block names 12 different row blocks; every row block is named by some column block.
All inputs are finite; a program needn't handle non-finite values.
Results may differ from a plain program's by a relative error of at most 0.001.
Values sent between devices are 32-bit elements; how exact they have to be, the bound alone decides.
A program may use at most 128 MiB of HBM per device.

v0:
```python
import math

import jax
import jax.numpy as jnp
from jax import lax
from jax.sharding import PartitionSpec as P


def shifted(shard, axis, by):
    size = lax.axis_size(axis)
    pairs = [(i, i + by) for i in range(size) if 0 <= i + by < size]
    return lax.ppermute(shard, axis, pairs)


def per_device(iterate, source, coupling, pair_rows, diag_pot, profile, regular, irregular):
    channels, columns_all = iterate.shape
    blocks_here = coupling.shape[0]
    pair_count = coupling.shape[1]
    block_size = coupling.shape[2]
    points = diag_pot.shape[1]
    num_sides = columns_all // points
    slab_count = lax.axis_size("slab")
    chan_count = lax.axis_size("chan")
    total_blocks = blocks_here * chan_count
    iterate_blocks = iterate.reshape(blocks_here, block_size, columns_all)
    products = jnp.einsum(
        "jpab,jbr->jpar", coupling, iterate_blocks, preferred_element_type=jnp.float32
    )
    products = products.reshape(blocks_here * pair_count, block_size, columns_all)
    targets = pair_rows.reshape(blocks_here * pair_count)
    row_sums = jax.ops.segment_sum(products, targets, num_segments=total_blocks)
    row_sums = row_sums.reshape(total_blocks * block_size, columns_all)
    coupled = lax.psum_scatter(row_sums, "chan", scatter_dimension=0, tiled=True)
    coupled = coupled.reshape(channels, points, num_sides)
    current = iterate.reshape(channels, points, num_sides).astype(jnp.float32)
    driving = diag_pot[:, :, None] * current + profile[None, :, None] * coupled
    quad_step = 1.0 / math.sqrt(points * slab_count)
    outward_terms = regular[:, :, None] * driving * quad_step
    inward_terms = irregular[:, :, None] * driving * quad_step
    outward_local = jnp.cumsum(outward_terms, axis=1)
    inward_incl = jnp.flip(jnp.cumsum(jnp.flip(inward_terms, 1), axis=1), 1)
    inward_local = inward_incl - inward_terms
    outward_total = jnp.transpose(outward_local[:, -1, :])
    inward_total = jnp.transpose(inward_incl[:, 0, :])
    empty_carry = jnp.zeros_like(outward_total)

    def relay_step(hop_index, carries):
        carry_out, carry_in = carries
        carry_out = shifted(carry_out + outward_total, "slab", 1)
        carry_in = shifted(carry_in + inward_total, "slab", -1)
        return (carry_out, carry_in)

    carry_out, carry_in = lax.fori_loop(0, slab_count - 1, relay_step, (empty_carry, empty_carry))
    outward = outward_local + jnp.transpose(carry_out)[:, None, :]
    inward = inward_local + jnp.transpose(carry_in)[:, None, :]
    updated = (
        source.astype(jnp.float32).reshape(channels, points, num_sides)
        + irregular[:, :, None] * outward
        + regular[:, :, None] * inward
    )
    return updated.reshape(channels, columns_all).astype(jnp.bfloat16)


def solution(mesh):
    placed = (
        P("chan", "slab"),
        P("chan", "slab"),
        P("chan", None, None, None),
        P("chan", None),
        P("chan", "slab"),
        P("slab"),
        P("chan", "slab"),
        P("chan", "slab"),
    )
    return jax.shard_map(
        per_device, mesh=mesh, in_specs=placed, out_specs=P("chan", "slab"), check_vma=False
    )
```

profile of v0, /device:TPU:1, one launch (start us, length us, event | category | flops | bytes accessed | tf_op | source)
XLA Modules:
  0.0 734.3 jit_solution(15569357602553363493)
XLA Ops:
  7.4 10.4 %fusion.15 = f32[24,12,128,128]{3,2,1,0:T(8,128)} fusion(bf16[24,12,128,128]{3,2,1,0:T(8,128)(2,1)} %param.12, bf16[24,128,128,1]{2,1,3,0:T(8,128)(2,1)} %bitcast.55), kind=kOutput, calls=%fused_computation.21 | convolution fusion | flops 1207959552 | bytes 29097984 | tf_op jit(solution)/shard_map/jpab,jbr->jpar/dot_general | solution.py:26
  24.0 59.8 %scatter_fusion = f32[192,128,128]{2,1,0:T(8,128)} fusion(f32[192,128,128]{2,1,0:T(8,128)} %broadcast_in_dim.4, s32[288]{0:T(512)S(1)} %reshape.40, f32[288,128,128]{2,1,0:T(8,128)} %bitcast.52), kind=kCustom, calls=%fused_computation | custom fusion | flops 4718592 | bytes 56624256 | tf_op jit(solution)/shard_map/scatter-add | solution.py:31
  83.8 12.6 %copy.15 = f32[24576,128]{0,1:T(8,128)} copy(f32[24576,128]{1,0:T(8,128)} %bitcast.51) | data formatting | bytes 25165824 | tf_op jit(solution)/shard_map/reshape | solution.py:32
  100.1 242.3 %reduce-scatter.2.cloned.1.call-done = f32[3072,128]{0,1:T(8,128)} async-done(((f32[24576,128]{0,1:T(8,128)}), f32[3072,128]{0,1:T(8,128)}) %reduce-scatter.2.cloned.1.call-update) | async-done | bytes 1572880 | tf_op jit(solution)/shard_map/reduce_scatter | solution.py:33
  349.8 370.8 %while.12 = (s32[]{:T(128)}, f32[8,3072]{1,0:T(8,128)S(1)}, f32[8,3072]{1,0:T(8,128)S(1)}, f32[8,3072]{1,0:T(8,128)S(1)}, f32[8,3072]{1,0:T(8,128)S(1)}, /*index=5*/s32[]{:T(128)}) while((s32[]{:T(128)}, f32[8,3072]{1,0:T(8,128)S(1)}, f32[8,3072]{1,0:T(8,128)S(1)}, f32[8,3072]{1,0:T(8,128)S(1)}, f32[8,3072]{1,0:T(8,128)S(1)}, ...), condition=%wide.region_5.6_spmd, body=%wide.region_4.5_spmd.sunk | while | flops 49154 | bytes 1376405 | solution.py:53
  397.4 8.2 %collective-permute-done.1 = f32[8,3072]{1,0:T(8,128)S(1)} collective-permute-done((f32[8,3072]{1,0:T(8,128)}, f32[8,3072]{1,0:T(8,128)S(1)}, u32[]{:S(2)}, u32[]{:S(2)}) %collective-permute-start.1) | collective-permute-done | bytes 98336 | tf_op jit(solution)/shard_map/while/body/eval_jaxpr/ppermute | solution.py:12
  411.3 6.3 collective-permute-done.1
  423.2 6.4 collective-permute-done.1
  435.2 6.5 collective-permute-done.1
  447.4 6.5 collective-permute-done.1
  459.5 6.5 collective-permute-done.1
  471.7 6.5 collective-permute-done.1
  483.8 6.5 collective-permute-done.1
  495.9 6.5 collective-permute-done.1
  508.0 6.5 collective-permute-done.1
  520.2 6.5 collective-permute-done.1
  532.3 6.5 collective-permute-done.1
  544.4 6.5 collective-permute-done.1
  556.5 6.5 collective-permute-done.1
  568.7 6.5 collective-permute-done.1
  580.8 6.5 collective-permute-done.1
  592.9 6.5 collective-permute-done.1
  605.0 6.5 collective-permute-done.1
  617.2 6.5 collective-permute-done.1
  629.3 6.5 collective-permute-done.1
  641.4 6.5 collective-permute-done.1
  653.5 6.5 collective-permute-done.1
  665.7 6.5 collective-permute-done.1
  677.8 6.5 collective-permute-done.1
  689.9 6.5 collective-permute-done.1
  702.0 6.5 collective-permute-done.1
  714.2 6.5 collective-permute-done.1
  (193 shorter events, 218.1 us)
Async XLA Ops:
  6.5 335.9 %reduce-scatter.2.cloned.1.call-start = ((), (), s32[]{:S(2)}) async-start(), calls=%async_computation.1 | async-start | bytes 14155776 | tf_op jit(solution)/shard_map/reduce_scatter | solution.py:33
  354.5 6.8 collective-permute-start.1
  364.6 6.1 collective-permute-start.1
  373.9 6.1 collective-permute-start.1
  383.3 8.5 %collective-permute-start.1 = (f32[8,3072]{1,0:T(8,128)}, f32[8,3072]{1,0:T(8,128)S(1)}, u32[]{:S(2)}, u32[]{:S(2)}) collective-permute-start(f32[8,3072]{1,0:T(8,128)} %add.82), channel_id=1, source_target_pairs={{8,0},{16,8},{24,16},{32,24},{40,32},{48,40},{56,48},{64,56},{72,6... | collective-permute-start | bytes 294920 | tf_op jit(solution)/shard_map/while/body/eval_jaxpr/ppermute | solution.py:12
  395.0 10.6 %collective-permute-start.1 = (f32[8,3072]{1,0:T(8,128)}, f32[8,3072]{1,0:T(8,128)S(1)}, u32[]{:S(2)}, u32[]{:S(2)}) collective-permute-start(f32[8,3072]{1,0:T(8,128)} %add.82), channel_id=1, source_target_pairs={{8,0},{16,8},{24,16},{32,24},{40,32},{48,40},{56,48},{64,56},{72,6... | collective-permute-start | bytes 294920 | tf_op jit(solution)/shard_map/while/body/eval_jaxpr/ppermute | solution.py:12
  408.9 8.7 %collective-permute-start.1 = (f32[8,3072]{1,0:T(8,128)}, f32[8,3072]{1,0:T(8,128)S(1)}, u32[]{:S(2)}, u32[]{:S(2)}) collective-permute-start(f32[8,3072]{1,0:T(8,128)} %add.82), channel_id=1, source_target_pairs={{8,0},{16,8},{24,16},{32,24},{40,32},{48,40},{56,48},{64,56},{72,6... | collective-permute-start | bytes 294920 | tf_op jit(solution)/shard_map/while/body/eval_jaxpr/ppermute | solution.py:12
  420.8 8.8 %collective-permute-start.1 = (f32[8,3072]{1,0:T(8,128)}, f32[8,3072]{1,0:T(8,128)S(1)}, u32[]{:S(2)}, u32[]{:S(2)}) collective-permute-start(f32[8,3072]{1,0:T(8,128)} %add.82), channel_id=1, source_target_pairs={{8,0},{16,8},{24,16},{32,24},{40,32},{48,40},{56,48},{64,56},{72,6... | collective-permute-start | bytes 294920 | tf_op jit(solution)/shard_map/while/body/eval_jaxpr/ppermute | solution.py:12
  432.8 9.0 %collective-permute-start.1 = (f32[8,3072]{1,0:T(8,128)}, f32[8,3072]{1,0:T(8,128)S(1)}, u32[]{:S(2)}, u32[]{:S(2)}) collective-permute-start(f32[8,3072]{1,0:T(8,128)} %add.82), channel_id=1, source_target_pairs={{8,0},{16,8},{24,16},{32,24},{40,32},{48,40},{56,48},{64,56},{72,6... | collective-permute-start | bytes 294920 | tf_op jit(solution)/shard_map/while/body/eval_jaxpr/ppermute | solution.py:12
  445.0 8.9 %collective-permute-start.1 = (f32[8,3072]{1,0:T(8,128)}, f32[8,3072]{1,0:T(8,128)S(1)}, u32[]{:S(2)}, u32[]{:S(2)}) collective-permute-start(f32[8,3072]{1,0:T(8,128)} %add.82), channel_id=1, source_target_pairs={{8,0},{16,8},{24,16},{32,24},{40,32},{48,40},{56,48},{64,56},{72,6... | collective-permute-start | bytes 294920 | tf_op jit(solution)/shard_map/while/body/eval_jaxpr/ppermute | solution.py:12
  457.1 8.9 %collective-permute-start.1 = (f32[8,3072]{1,0:T(8,128)}, f32[8,3072]{1,0:T(8,128)S(1)}, u32[]{:S(2)}, u32[]{:S(2)}) collective-permute-start(f32[8,3072]{1,0:T(8,128)} %add.82), channel_id=1, source_target_pairs={{8,0},{16,8},{24,16},{32,24},{40,32},{48,40},{56,48},{64,56},{72,6... | collective-permute-start | bytes 294920 | tf_op jit(solution)/shard_map/while/body/eval_jaxpr/ppermute | solution.py:12
  469.3 8.9 %collective-permute-start.1 = (f32[8,3072]{1,0:T(8,128)}, f32[8,3072]{1,0:T(8,128)S(1)}, u32[]{:S(2)}, u32[]{:S(2)}) collective-permute-start(f32[8,3072]{1,0:T(8,128)} %add.82), channel_id=1, source_target_pairs={{8,0},{16,8},{24,16},{32,24},{40,32},{48,40},{56,48},{64,56},{72,6... | collective-permute-start | bytes 294920 | tf_op jit(solution)/shard_map/while/body/eval_jaxpr/ppermute | solution.py:12
  481.4 8.9 %collective-permute-start.1 = (f32[8,3072]{1,0:T(8,128)}, f32[8,3072]{1,0:T(8,128)S(1)}, u32[]{:S(2)}, u32[]{:S(2)}) collective-permute-start(f32[8,3072]{1,0:T(8,128)} %add.82), channel_id=1, source_target_pairs={{8,0},{16,8},{24,16},{32,24},{40,32},{48,40},{56,48},{64,56},{72,6... | collective-permute-start | bytes 294920 | tf_op jit(solution)/shard_map/while/body/eval_jaxpr/ppermute | solution.py:12
  493.5 8.9 %collective-permute-start.1 = (f32[8,3072]{1,0:T(8,128)}, f32[8,3072]{1,0:T(8,128)S(1)}, u32[]{:S(2)}, u32[]{:S(2)}) collective-permute-start(f32[8,3072]{1,0:T(8,128)} %add.82), channel_id=1, source_target_pairs={{8,0},{16,8},{24,16},{32,24},{40,32},{48,40},{56,48},{64,56},{72,6... | collective-permute-start | bytes 294920 | tf_op jit(solution)/shard_map/while/body/eval_jaxpr/ppermute | solution.py:12
  505.6 8.9 %collective-permute-start.1 = (f32[8,3072]{1,0:T(8,128)}, f32[8,3072]{1,0:T(8,128)S(1)}, u32[]{:S(2)}, u32[]{:S(2)}) collective-permute-start(f32[8,3072]{1,0:T(8,128)} %add.82), channel_id=1, source_target_pairs={{8,0},{16,8},{24,16},{32,24},{40,32},{48,40},{56,48},{64,56},{72,6... | collective-permute-start | bytes 294920 | tf_op jit(solution)/shard_map/while/body/eval_jaxpr/ppermute | solution.py:12
  517.8 8.9 %collective-permute-start.1 = (f32[8,3072]{1,0:T(8,128)}, f32[8,3072]{1,0:T(8,128)S(1)}, u32[]{:S(2)}, u32[]{:S(2)}) collective-permute-start(f32[8,3072]{1,0:T(8,128)} %add.82), channel_id=1, source_target_pairs={{8,0},{16,8},{24,16},{32,24},{40,32},{48,40},{56,48},{64,56},{72,6... | collective-permute-start | bytes 294920 | tf_op jit(solution)/shard_map/while/body/eval_jaxpr/ppermute | solution.py:12
  529.9 8.9 %collective-permute-start.1 = (f32[8,3072]{1,0:T(8,128)}, f32[8,3072]{1,0:T(8,128)S(1)}, u32[]{:S(2)}, u32[]{:S(2)}) collective-permute-start(f32[8,3072]{1,0:T(8,128)} %add.82), channel_id=1, source_target_pairs={{8,0},{16,8},{24,16},{32,24},{40,32},{48,40},{56,48},{64,56},{72,6... | collective-permute-start | bytes 294920 | tf_op jit(solution)/shard_map/while/body/eval_jaxpr/ppermute | solution.py:12
  542.0 8.9 %collective-permute-start.1 = (f32[8,3072]{1,0:T(8,128)}, f32[8,3072]{1,0:T(8,128)S(1)}, u32[]{:S(2)}, u32[]{:S(2)}) collective-permute-start(f32[8,3072]{1,0:T(8,128)} %add.82), channel_id=1, source_target_pairs={{8,0},{16,8},{24,16},{32,24},{40,32},{48,40},{56,48},{64,56},{72,6... | collective-permute-start | bytes 294920 | tf_op jit(solution)/shard_map/while/body/eval_jaxpr/ppermute | solution.py:12
  554.1 8.9 %collective-permute-start.1 = (f32[8,3072]{1,0:T(8,128)}, f32[8,3072]{1,0:T(8,128)S(1)}, u32[]{:S(2)}, u32[]{:S(2)}) collective-permute-start(f32[8,3072]{1,0:T(8,128)} %add.82), channel_id=1, source_target_pairs={{8,0},{16,8},{24,16},{32,24},{40,32},{48,40},{56,48},{64,56},{72,6... | collective-permute-start | bytes 294920 | tf_op jit(solution)/shard_map/while/body/eval_jaxpr/ppermute | solution.py:12
  566.3 8.9 %collective-permute-start.1 = (f32[8,3072]{1,0:T(8,128)}, f32[8,3072]{1,0:T(8,128)S(1)}, u32[]{:S(2)}, u32[]{:S(2)}) collective-permute-start(f32[8,3072]{1,0:T(8,128)} %add.82), channel_id=1, source_target_pairs={{8,0},{16,8},{24,16},{32,24},{40,32},{48,40},{56,48},{64,56},{72,6... | collective-permute-start | bytes 294920 | tf_op jit(solution)/shard_map/while/body/eval_jaxpr/ppermute | solution.py:12
  578.4 8.9 %collective-permute-start.1 = (f32[8,3072]{1,0:T(8,128)}, f32[8,3072]{1,0:T(8,128)S(1)}, u32[]{:S(2)}, u32[]{:S(2)}) collective-permute-start(f32[8,3072]{1,0:T(8,128)} %add.82), channel_id=1, source_target_pairs={{8,0},{16,8},{24,16},{32,24},{40,32},{48,40},{56,48},{64,56},{72,6... | collective-permute-start | bytes 294920 | tf_op jit(solution)/shard_map/while/body/eval_jaxpr/ppermute | solution.py:12
  590.5 8.9 %collective-permute-start.1 = (f32[8,3072]{1,0:T(8,128)}, f32[8,3072]{1,0:T(8,128)S(1)}, u32[]{:S(2)}, u32[]{:S(2)}) collective-permute-start(f32[8,3072]{1,0:T(8,128)} %add.82), channel_id=1, source_target_pairs={{8,0},{16,8},{24,16},{32,24},{40,32},{48,40},{56,48},{64,56},{72,6... | collective-permute-start | bytes 294920 | tf_op jit(solution)/shard_map/while/body/eval_jaxpr/ppermute | solution.py:12
  602.6 8.9 %collective-permute-start.1 = (f32[8,3072]{1,0:T(8,128)}, f32[8,3072]{1,0:T(8,128)S(1)}, u32[]{:S(2)}, u32[]{:S(2)}) collective-permute-start(f32[8,3072]{1,0:T(8,128)} %add.82), channel_id=1, source_target_pairs={{8,0},{16,8},{24,16},{32,24},{40,32},{48,40},{56,48},{64,56},{72,6... | collective-permute-start | bytes 294920 | tf_op jit(solution)/shard_map/while/body/eval_jaxpr/ppermute | solution.py:12
  614.8 8.9 %collective-permute-start.1 = (f32[8,3072]{1,0:T(8,128)}, f32[8,3072]{1,0:T(8,128)S(1)}, u32[]{:S(2)}, u32[]{:S(2)}) collective-permute-start(f32[8,3072]{1,0:T(8,128)} %add.82), channel_id=1, source_target_pairs={{8,0},{16,8},{24,16},{32,24},{40,32},{48,40},{56,48},{64,56},{72,6... | collective-permute-start | bytes 294920 | tf_op jit(solution)/shard_map/while/body/eval_jaxpr/ppermute | solution.py:12
  626.9 8.9 %collective-permute-start.1 = (f32[8,3072]{1,0:T(8,128)}, f32[8,3072]{1,0:T(8,128)S(1)}, u32[]{:S(2)}, u32[]{:S(2)}) collective-permute-start(f32[8,3072]{1,0:T(8,128)} %add.82), channel_id=1, source_target_pairs={{8,0},{16,8},{24,16},{32,24},{40,32},{48,40},{56,48},{64,56},{72,6... | collective-permute-start | bytes 294920 | tf_op jit(solution)/shard_map/while/body/eval_jaxpr/ppermute | solution.py:12
  639.0 8.9 %collective-permute-start.1 = (f32[8,3072]{1,0:T(8,128)}, f32[8,3072]{1,0:T(8,128)S(1)}, u32[]{:S(2)}, u32[]{:S(2)}) collective-permute-start(f32[8,3072]{1,0:T(8,128)} %add.82), channel_id=1, source_target_pairs={{8,0},{16,8},{24,16},{32,24},{40,32},{48,40},{56,48},{64,56},{72,6... | collective-permute-start | bytes 294920 | tf_op jit(solution)/shard_map/while/body/eval_jaxpr/ppermute | solution.py:12
  651.1 8.9 %collective-permute-start.1 = (f32[8,3072]{1,0:T(8,128)}, f32[8,3072]{1,0:T(8,128)S(1)}, u32[]{:S(2)}, u32[]{:S(2)}) collective-permute-start(f32[8,3072]{1,0:T(8,128)} %add.82), channel_id=1, source_target_pairs={{8,0},{16,8},{24,16},{32,24},{40,32},{48,40},{56,48},{64,56},{72,6... | collective-permute-start | bytes 294920 | tf_op jit(solution)/shard_map/while/body/eval_jaxpr/ppermute | solution.py:12
  663.3 8.9 %collective-permute-start.1 = (f32[8,3072]{1,0:T(8,128)}, f32[8,3072]{1,0:T(8,128)S(1)}, u32[]{:S(2)}, u32[]{:S(2)}) collective-permute-start(f32[8,3072]{1,0:T(8,128)} %add.82), channel_id=1, source_target_pairs={{8,0},{16,8},{24,16},{32,24},{40,32},{48,40},{56,48},{64,56},{72,6... | collective-permute-start | bytes 294920 | tf_op jit(solution)/shard_map/while/body/eval_jaxpr/ppermute | solution.py:12
  675.4 8.9 %collective-permute-start.1 = (f32[8,3072]{1,0:T(8,128)}, f32[8,3072]{1,0:T(8,128)S(1)}, u32[]{:S(2)}, u32[]{:S(2)}) collective-permute-start(f32[8,3072]{1,0:T(8,128)} %add.82), channel_id=1, source_target_pairs={{8,0},{16,8},{24,16},{32,24},{40,32},{48,40},{56,48},{64,56},{72,6... | collective-permute-start | bytes 294920 | tf_op jit(solution)/shard_map/while/body/eval_jaxpr/ppermute | solution.py:12
  687.5 8.9 %collective-permute-start.1 = (f32[8,3072]{1,0:T(8,128)}, f32[8,3072]{1,0:T(8,128)S(1)}, u32[]{:S(2)}, u32[]{:S(2)}) collective-permute-start(f32[8,3072]{1,0:T(8,128)} %add.82), channel_id=1, source_target_pairs={{8,0},{16,8},{24,16},{32,24},{40,32},{48,40},{56,48},{64,56},{72,6... | collective-permute-start | bytes 294920 | tf_op jit(solution)/shard_map/while/body/eval_jaxpr/ppermute | solution.py:12
  699.6 8.9 %collective-permute-start.1 = (f32[8,3072]{1,0:T(8,128)}, f32[8,3072]{1,0:T(8,128)S(1)}, u32[]{:S(2)}, u32[]{:S(2)}) collective-permute-start(f32[8,3072]{1,0:T(8,128)} %add.82), channel_id=1, source_target_pairs={{8,0},{16,8},{24,16},{32,24},{40,32},{48,40},{56,48},{64,56},{72,6... | collective-permute-start | bytes 294920 | tf_op jit(solution)/shard_map/while/body/eval_jaxpr/ppermute | solution.py:12
  711.8 8.9 %collective-permute-start.1 = (f32[8,3072]{1,0:T(8,128)}, f32[8,3072]{1,0:T(8,128)S(1)}, u32[]{:S(2)}, u32[]{:S(2)}) collective-permute-start(f32[8,3072]{1,0:T(8,128)} %add.82), channel_id=1, source_target_pairs={{8,0},{16,8},{24,16},{32,24},{40,32},{48,40},{56,48},{64,56},{72,6... | collective-permute-start | bytes 294920 | tf_op jit(solution)/shard_map/while/body/eval_jaxpr/ppermute | solution.py:12
  (40 other events, 897.5 us)
Sparse Core Ops, SparseCore 0:
  96.5 245.8 reduce-scatter.1
where the time goes:
time: 743 us; the launch traced here: 734 us
  waiting for transfers between devices  438 us (59%)
  starting transfers between devices  134 us (18%)
  other arithmetic  109 us (15%)
  local copies, waits for them, and re-layouts  29 us (4%)
  between operations  13.5 us (2%)
  matrix products  10.4 us (1%)
    reduce_scatter x1, waiting for transfers between devices, per_device(): lax.psum_scatter(row_sums, 'chan', scatter_dimension=0, tiled=True)  242 us
    ppermute x62, waiting for transfers between devices, shifted(): return lax.ppermute(shard, axis, pairs)  195 us
    ppermute x62, starting transfers between devices, shifted(): return lax.ppermute(shard, axis, pairs)  134 us
    scatter-add x1, other arithmetic, per_device(): row_sums = jax.ops.segment_sum(products, targets, num_segments=total_blocks)  59.8 us
    add x31, other arithmetic, relay_step(): carry_out = shifted(carry_out + outward_total, 'slab', 1)  20.2 us
    add x31, other arithmetic, relay_step(): carry_in = shifted(carry_in + inward_total, 'slab', -1)  20.1 us
  transfers between devices with their start and end apart: 63, of which 32 were waited for; matrix products, arithmetic and copies ran while one was open for 3% of the time, Pallas kernels for 0%

commit v1 on v0

v1 whole, which is shorter than its diff:
```python
import math

import jax
import jax.numpy as jnp
from jax import lax
from jax.experimental import pallas as pl
from jax.experimental.pallas import tpu as pltpu
from jax.sharding import PartitionSpec as P

Y, ZL, CORES, ZH, X = 4, 4, 2, 2, 4
PLANE = ZL * CORES
BS = 128
BLOCKS = 24
PAIRS = 12
ROW_BLOCKS = 192
POINTS = 16
SIDES = 8
STEPS = 12
HALF = 6
ZERO_BLOCK = BLOCKS * PAIRS
HIGH = lax.Precision.HIGHEST
MESH = pl.DeviceIdType.MESH
F32 = jnp.float32


def dot0(a, b):
    return lax.dot_general(a, b, (((0,), (0,)), ((), ())), precision=HIGH, preferred_element_type=F32)


def dot1(a, b):
    return lax.dot_general(a, b, (((1,), (1,)), ((), ())), precision=HIGH, preferred_element_type=F32)


def iota(shape, dim):
    return lax.broadcasted_iota(jnp.int32, shape, dim)


def sweep(
    table, coup_hbm, iter_hbm, src_hbm, diag_hbm, prof, reg_hbm, irr_hbm, out,
    coup, itv, src, diag, reg, irr,
    part, rl_p, rl_m, own_p, own_m, cb_p, cb_m, z_out, z_in,
    drv0, reg_e, irr_e, out_l, in_l, p1, p2,
    in_sem, x_send, x_recv, z_send, z_recv, p1_send, p1_recv, p2_send, p2_recv,
):
    slab = lax.axis_index("slab")
    chan = lax.axis_index("chan")
    y = slab // PLANE
    spot = slab % PLANE
    zh = chan // X
    x = chan % X
    x_next, x_last, x_over = (x + 1) % X, (x + 3) % X, (x + 2) % X
    to_next = {"chan": zh * X + x_next}
    to_last = {"chan": zh * X + x_last}
    to_z = {"chan": (1 - zh) * X + x}

    loads = [
        pltpu.make_async_copy(coup_hbm, coup.at[pl.ds(0, ZERO_BLOCK)], in_sem.at[0]),
        pltpu.make_async_copy(iter_hbm, itv, in_sem.at[1]),
        pltpu.make_async_copy(diag_hbm, diag, in_sem.at[2]),
        pltpu.make_async_copy(reg_hbm, reg, in_sem.at[3]),
        pltpu.make_async_copy(irr_hbm, irr, in_sem.at[4]),
        pltpu.make_async_copy(src_hbm, src, in_sem.at[5]),
    ]
    for load in loads:
        load.start()
    coup[ZERO_BLOCK] = jnp.zeros((BS, BS), jnp.bfloat16)

    barrier = pltpu.get_barrier_semaphore()
    for peer in (to_next, to_last, to_z):
        pl.semaphore_signal(barrier, inc=1, device_id=peer, device_id_type=MESH)
    for hop in range(1, PLANE):
        peer = {"slab": y * PLANE + (spot + hop) % PLANE}
        pl.semaphore_signal(barrier, inc=1, device_id=peer, device_id_type=MESH)
    for hop in range(1, Y):
        peer = {"slab": ((y + hop) % Y) * PLANE + spot}
        pl.semaphore_signal(barrier, inc=1, device_id=peer, device_id_type=MESH)

    def dest(step, x_of):
        z_of = jnp.where(step < HALF, 1 - zh, zh)
        return (z_of * X + x_of) * BLOCKS

    def lower(step, x_of):
        return dest(step, x_of) + 2 * (step % HALF)

    def upper(step, x_of):
        return lower(step, x_of) + BLOCKS // 2

    def remote(src_ref, dst_ref, send, recv, peer):
        return pltpu.make_async_remote_copy(
            src_ref=src_ref, dst_ref=dst_ref, send_sem=send, recv_sem=recv,
            device_id=peer, device_id_type=MESH,
        )

    def x_copy(kind, step):
        src_row, landing, peer = (
            (lower(step, x_over), rl_p, to_next),
            (upper(step, x_over), rl_m, to_last),
            (upper(step, x_next), own_p, to_next),
            (lower(step, x_last), own_m, to_last),
            (lower(step, x_next), cb_p, to_next),
            (upper(step, x_last), cb_m, to_last),
        )[kind]
        return remote(
            part.at[pl.ds(src_row, 2)], landing.at[step],
            x_send.at[kind, step], x_recv.at[kind, step], peer,
        )

    def z_copy(piece):
        return remote(z_out.at[piece], z_in.at[piece], z_send.at[piece], z_recv.at[piece], to_z)

    def p1_copy(piece, hop):
        peer = {"slab": y * PLANE + (spot + hop) % PLANE}
        return remote(
            p1.at[piece, spot], p1.at[piece, spot],
            p1_send.at[piece, hop], p1_recv.at[piece, spot], peer,
        )

    def p1_arrival(piece, hop):
        whose = (spot + hop) % PLANE
        peer = {"slab": y * PLANE + whose}
        return remote(
            p1.at[piece, whose], p1.at[piece, whose],
            p1_send.at[piece, hop], p1_recv.at[piece, whose], peer,
        )

    def p2_copy(piece, hop):
        peer = {"slab": ((y + hop) % Y) * PLANE + spot}
        return remote(
            p2.at[piece, y], p2.at[piece, y],
            p2_send.at[piece, hop], p2_recv.at[piece, y], peer,
        )

    def p2_arrival(piece, hop):
        whose = (y + hop) % Y
        peer = {"slab": whose * PLANE + spot}
        return remote(
            p2.at[piece, whose], p2.at[piece, whose],
            p2_send.at[piece, hop], p2_recv.at[piece, whose], peer,
        )

    def multiply(row_a, row_b):
        rows = (row_a, row_a + 1, row_b, row_b + 1)
        total = jnp.zeros((4 * BS, BS), F32)
        for pair in range(BLOCKS // 2):
            left = jnp.concatenate(
                [
                    jnp.concatenate(
                        [coup[table[(2 * pair + k) * ROW_BLOCKS + row]] for k in range(2)], axis=1
                    )
                    for row in rows
                ],
                axis=0,
            )
            right = itv[pl.ds(pair * 2 * BS, 2 * BS), :]
            total = total + jnp.dot(left, right, preferred_element_type=F32)
        part[pl.ds(row_a, 2)] = total[: 2 * BS].reshape(2, BS, BS)
        part[pl.ds(row_b, 2)] = total[2 * BS :].reshape(2, BS, BS)

    spread = (iota((POINTS, BS), 1) // SIDES == iota((POINTS, BS), 0)).astype(F32)
    sides = (iota((SIDES, BS), 1) % SIDES == iota((SIDES, BS), 0)).astype(F32)
    from_n, to_n = iota((BS, BS), 0), iota((BS, BS), 1)
    same_side = from_n % SIDES == to_n % SIDES
    upto = (same_side & (from_n // SIDES <= to_n // SIDES)).astype(F32)
    above = (same_side & (from_n // SIDES > to_n // SIDES)).astype(F32)
    prof_e = dot0(prof[...], spread)
    quad_step = 1.0 / math.sqrt(POINTS * Y * PLANE)

    def columns(piece, half):
        return pl.ds(pl.multiple_of(piece * 2 * BS + half * (BLOCKS // 2) * BS, 2 * BS), 2 * BS)

    def blocks(piece, half):
        return pl.ds(2 * piece + half * (BLOCKS // 2), 2)

    def expand(piece):
        for half in range(2):
            cols, rows = columns(piece, half), blocks(piece, half)
            shape = (2, BS, BS)
            reg_e[rows] = dot0(reg[:, cols], spread).reshape(shape)
            irr_e[rows] = dot0(irr[:, cols], spread).reshape(shape)
            now = itv[cols, :].astype(F32)
            drv0[rows] = (dot0(diag[:, cols], spread) * now).reshape(shape)

    def combine(step):
        for kind, landing in ((0, rl_p), (1, rl_m)):
            x_copy(kind, step).wait_recv()
        lo, hi = pl.ds(lower(step, x_next), 2), pl.ds(upper(step, x_last), 2)
        part[lo] = part[lo] + rl_p[step]
        x_copy(4, step).start()
        part[hi] = part[hi] + rl_m[step]
        x_copy(5, step).start()

    def sums(step):
        for kind in (2, 3, 4, 5):
            x_copy(kind, step).wait_recv()
        lo = part[pl.ds(lower(step, x), 2)] + cb_p[step] + own_m[step]
        hi = part[pl.ds(upper(step, x), 2)] + own_p[step] + cb_m[step]
        return lo, hi

    def finish_far(step):
        lo, hi = sums(step)
        z_out[step, pl.ds(0, 2)] = lo
        z_out[step, pl.ds(2, 2)] = hi
        z_copy(step).start()

    def finish_near(step):
        piece = step - HALF
        z_copy(piece).wait_recv()
        both = sums(step)
        for half in range(2):
            rows = blocks(piece, half)
            coupled = both[half] + z_in[piece, pl.ds(2 * half, 2)]
            driving = (drv0[rows] + prof_e * coupled) * quad_step
            outs = (reg_e[rows] * driving).reshape(2 * BS, BS)
            ins = (irr_e[rows] * driving).reshape(2 * BS, BS)
            cols = pl.ds(half * 2 * BS, 2 * BS)
            p1[piece, spot, pl.ds(0, SIDES), cols] = dot1(sides, outs)
            p1[piece, spot, pl.ds(SIDES, SIDES), cols] = dot1(sides, ins)
            out_l[rows] = jnp.dot(outs, upto, precision=HIGH, preferred_element_type=F32).reshape(2, BS, BS)
            in_l[rows] = jnp.dot(ins, above, precision=HIGH, preferred_element_type=F32).reshape(2, BS, BS)
        for hop in range(1, PLANE):
            p1_copy(piece, hop).start()

    def plane_sum(piece):
        for hop in range(1, PLANE):
            p1_arrival(piece, hop).wait_recv()
        total = p1[piece, 0]
        for whose in range(1, PLANE):
            total = total + p1[piece, whose]
        p2[piece, y] = total
        for hop in range(1, Y):
            p2_copy(piece, hop).start()

    def emit(piece):
        for hop in range(1, Y):
            p2_arrival(piece, hop).wait_recv()
        before = jnp.zeros((SIDES, 4 * BS), F32)
        after = jnp.zeros((SIDES, 4 * BS), F32)
        for whose in range(PLANE):
            before = before + jnp.where(whose < spot, p1[piece, whose, pl.ds(0, SIDES)], 0.0)
            after = after + jnp.where(whose > spot, p1[piece, whose, pl.ds(SIDES, SIDES)], 0.0)
        for whose in range(Y):
            before = before + jnp.where(whose < y, p2[piece, whose, pl.ds(0, SIDES)], 0.0)
            after = after + jnp.where(whose > y, p2[piece, whose, pl.ds(SIDES, SIDES)], 0.0)
        for half in range(2):
            rows = blocks(piece, half)
            take = slice(half * 2 * BS, (half + 1) * 2 * BS)
            outward = out_l[rows] + dot0(before[:, take], sides).reshape(2, BS, BS)
            inward = in_l[rows] + dot0(after[:, take], sides).reshape(2, BS, BS)
            updated = src[rows].astype(F32) + irr_e[rows] * outward + reg_e[rows] * inward
            out[rows] = updated.astype(jnp.bfloat16)

    loads[0].wait()
    loads[1].wait()
    pl.semaphore_wait(barrier, 3 + (PLANE - 1) + (Y - 1))

    def one_step(step, _):
        @pl.when(step < STEPS)
        def _():
            multiply(lower(step, x_over), upper(step, x_over))
            x_copy(0, step).start()
            x_copy(1, step).start()

        @pl.when((step >= 1) & (step <= STEPS))
        def _():
            combine(step - 1)

        @pl.when(step < STEPS)
        def _():
            multiply(upper(step, x_next), lower(step, x_last))
            x_copy(2, step).start()
            x_copy(3, step).start()

        @pl.when((step >= 2) & (step < HALF + 2))
        def _():
            finish_far(step - 2)

        @pl.when(step >= HALF + 2)
        def _():
            @pl.when(step < STEPS + 2)
            def _():
                finish_near(step - 2)

        @pl.when(step < STEPS)
        def _():
            multiply(lower(step, x_next), upper(step, x_last))
            multiply(lower(step, x), upper(step, x))

        @pl.when(step == 0)
        def _():
            for load in loads[2:]:
                load.wait()

        @pl.when(step < HALF)
        def _():
            expand(step)

        @pl.when((step >= HALF + 3) & (step < STEPS + 3))
        def _():
            plane_sum(step - HALF - 3)

        @pl.when(step >= HALF + 4)
        def _():
            emit(step - HALF - 4)

        return 0

    lax.fori_loop(0, STEPS + 4, one_step, 0)

    def drain(step, _):
        for kind in range(6):
            x_copy(kind, step).wait_send()
        return 0

    lax.fori_loop(0, STEPS, drain, 0)

    def drain_pieces(piece, _):
        z_copy(piece).wait_send()
        for hop in range(1, PLANE):
            p1_copy(piece, hop).wait_send()
        for hop in range(1, Y):
            p2_copy(piece, hop).wait_send()
        return 0

    lax.fori_loop(0, HALF, drain_pieces, 0)


def per_device(iterate, source, coupling, pair_rows, diag_pot, profile, regular, irregular):
    channels = iterate.shape[0]
    pair_index = jnp.arange(BLOCKS * PAIRS, dtype=jnp.int32).reshape(BLOCKS, PAIRS, 1)
    named = pair_rows[:, :, None] == jnp.arange(ROW_BLOCKS, dtype=jnp.int32)
    table = ZERO_BLOCK + jnp.sum(jnp.where(named, pair_index - ZERO_BLOCK, 0), axis=1)
    anywhere = pl.BlockSpec(memory_space=pl.ANY)
    vmem = pl.BlockSpec(memory_space=pltpu.VMEM)
    blocked = (BLOCKS, BS, BS)
    landing = pltpu.VMEM((STEPS, 2, BS, BS), F32)
    dma = pltpu.SemaphoreType.DMA
    out = pl.pallas_call(
        sweep,
        out_shape=jax.ShapeDtypeStruct(blocked, jnp.bfloat16),
        in_specs=[pl.BlockSpec(memory_space=pltpu.SMEM)] + [anywhere] * 4 + [vmem] + [anywhere] * 2,
        out_specs=vmem,
        scratch_shapes=[
            pltpu.VMEM((ZERO_BLOCK + 1, BS, BS), jnp.bfloat16),
            pltpu.VMEM((channels, BS), jnp.bfloat16),
            pltpu.VMEM(blocked, jnp.bfloat16),
            pltpu.VMEM((POINTS, channels), F32),
            pltpu.VMEM((POINTS, channels), F32),
            pltpu.VMEM((POINTS, channels), F32),
            pltpu.VMEM((ROW_BLOCKS, BS, BS), F32),
            landing, landing, landing, landing, landing, landing,
            pltpu.VMEM((HALF, 4, BS, BS), F32),
            pltpu.VMEM((HALF, 4, BS, BS), F32),
            pltpu.VMEM(blocked, F32),
            pltpu.VMEM(blocked, F32),
            pltpu.VMEM(blocked, F32),
            pltpu.VMEM(blocked, F32),
            pltpu.VMEM(blocked, F32),
            pltpu.VMEM((HALF, PLANE, 2 * SIDES, 4 * BS), F32),
            pltpu.VMEM((HALF, Y, 2 * SIDES, 4 * BS), F32),
            dma((6,)),
            dma((6, STEPS)), dma((6, STEPS)),
            dma((HALF,)), dma((HALF,)),
            dma((HALF, PLANE)), dma((HALF, PLANE)),
            dma((HALF, Y)), dma((HALF, Y)),
        ],
        compiler_params=pltpu.CompilerParams(
            collective_id=0, has_side_effects=True, vmem_limit_bytes=60 * 2**20
        ),
        name="sweep",
    )(
        table.reshape(-1),
        coupling.reshape(BLOCKS * PAIRS, BS, BS),
        iterate,
        source.reshape(blocked),
        diag_pot.T,
        profile.reshape(POINTS, 1),
        regular.T,
        irregular.T,
    )
    return out.reshape(channels, BS)


def solution(mesh):
    placed = (
        P("chan", "slab"),
        P("chan", "slab"),
        P("chan", None, None, None),
        P("chan", None),
        P("chan", "slab"),
        P("slab"),
        P("chan", "slab"),
        P("chan", "slab"),
    )
    return jax.shard_map(
        per_device, mesh=mesh, in_specs=placed, out_specs=P("chan", "slab"), check_vma=False
    )
```

time: 743 us -> 143 us (0.19); the launches traced: 734 us -> 143 us
  waiting for transfers between devices: 438 us -> 0 us
  Pallas kernels: 0 us -> 138 us
  starting transfers between devices: 134 us -> 0 us
  other arithmetic: 109 us -> 0.85 us
  local copies, waits for them, and re-layouts: 29 us -> 4.07 us
  between operations: 13.5 us -> 0.02 us
  matrix products: 10.4 us -> 0 us
    reduce_scatter x1 -> x0, waiting for transfers between devices: 242 us -> none  [per_device(): lax.psum_scatter(row_sums, 'chan', scatter_dimension=0, tiled=True)]
    ppermute x62 -> x0, waiting for transfers between devices: 195 us -> none  [shifted(): return lax.ppermute(shard, axis, pairs)]
    pallas_call x0 -> x1, Pallas kernels: none -> 138 us  [per_device(): pl.pallas_call(sweep, out_shape=jax.ShapeDtypeStruct(blocked, jnp.bfloat1...]
    ppermute x62 -> x0, starting transfers between devices: 134 us -> none  [shifted(): return lax.ppermute(shard, axis, pairs)]
    scatter-add x1 -> x0, other arithmetic: 59.8 us -> none  [per_device(): row_sums = jax.ops.segment_sum(products, targets, num_segments=total_blocks)]
    add x62 -> x1, other arithmetic: 40.3 us -> 0.01 us  [per_device(): ZERO_BLOCK + jnp.sum(jnp.where(named, pair_index - ZERO_BLOCK, 0), axis=1)]
    reshape x2 -> x1, local copies, waits for them, and re-layouts: 14.1 us -> 1.32 us  [per_device(): profile.reshape(POINTS, 1)]
    dot_general x1 -> x0, matrix products: 10.4 us -> none  [per_device(): jnp.einsum('jpab,jbr->jpar', coupling, iterate_blocks, preferred_element_...]
  transfers between devices with their start and end apart: 63 -> 0, of which waited for: 32 -> 0; matrix products, arithmetic and copies ran while one was open for 3% -> 0% of each run, Pallas kernels for 0% -> 0%
where the time goes in v1:
time: 143 us
  Pallas kernels  138 us (97%)
  local copies, waits for them, and re-layouts  4.07 us (3%)
    pallas_call x1, Pallas kernels, per_device(): pl.pallas_call(sweep, out_shape=jax.ShapeDtypeStruct(blocked, jnp.bfloat1...  138 us

profile of v1, /device:TPU:1, one launch (start us, length us, event | category | flops | bytes accessed | tf_op | source)
XLA Modules:
  0.0 142.9 jit_solution(16082040430133668969)
XLA Ops:
  0.0 1.3 copy.11.prof
  1.3 0.8 select_reduce_fusion
  2.2 0.7 add.24.table
  2.9 138.0 %sweep.1 = bf16[24,128,128]{2,1,0:T(8,128)(2,1)} custom-call(s32[4608]{0:T(1024)} %add.24.table, bf16[288,128,128]{2,1,0:T(8,128)(2,1)} %bitcast.7, bf16[3072,128]{1,0:T(8,128)(2,1)} %iter_hbm.1, bf16[24,128,128]{2,1,0:T(8,128)(2,1)} %bitcast.9, f32[16,3072]{1,0:T(8,128)} %bitcast.10, f32[16,1]{1,0:T(8,128)} %copy.11.prof, f32[16,3072]{1,0:T(8,128)} %bitcast.11, ...), custom_call_target="tpu_custom_call" | custom-call | tf_op jit(solution)/shard_map/sweep/pallas_call | solution.py:337
  140.9 2.1 %copy.13 = bf16[3072,128]{1,0:T(8,128)(2,1)} copy(bf16[3072,128]{1,0:T(8,128)(2,1)} %bitcast.8) | data formatting | bytes 1572864
  (2 shorter events, 0.0 us)

commit v2 on v0

v2 whole, which is shorter than its diff:
```python
import math

import jax
import jax.numpy as jnp
from jax import lax
from jax.experimental import pallas as pl
from jax.experimental.pallas import tpu as pltpu
from jax.sharding import PartitionSpec as P

Y, ZL, CORES, ZH, X = 4, 4, 2, 2, 4
PLANE = ZL * CORES
BS = 128
BLOCKS = 24
PAIRS = 12
ROW_BLOCKS = 192
POINTS = 16
SIDES = 8
CHANNELS = BLOCKS * BS
HALF_ROWS = CHANNELS // 2
STEPS = 12
HALF = 6
PIECE = 256
TAIL = ((1280, 128), (1408, 64), (1472, 64))
SENDS = STEPS - 1 + len(TAIL)
LOADS = 4
SHARE = BLOCKS * PAIRS // LOADS
HIGH = lax.Precision.HIGHEST
MESH = pl.DeviceIdType.MESH
F32 = jnp.float32


def dot0(a, b):
    return lax.dot_general(a, b, (((0,), (0,)), ((), ())), precision=HIGH, preferred_element_type=F32)


def dot1(a, b):
    return lax.dot_general(a, b, (((1,), (1,)), ((), ())), precision=HIGH, preferred_element_type=F32)


def iota(shape, dim):
    return lax.broadcasted_iota(jnp.int32, shape, dim)


def sweep(
    pairs, coup_hbm, iter_hbm, src_hbm, diag_hbm, prof_hbm, reg_hbm, irr_hbm, out_hbm,
    square, prof, table_v, table, coup_0, coup_1, coup_2, coup_3, itv, src, diag, reg, irr, out,
    part, relayed, arrived, z_out, z_in,
    drv0, reg_e, irr_e, local, own_0, own_1, own_2, near_0, near_1, near_2,
    in_sem, out_sem, x_send, x_recv, z_send, z_recv,
    scan_send, scan_recv,
):
    slab = lax.axis_index("slab")
    chan = lax.axis_index("chan")
    y = slab // PLANE
    spot = slab % PLANE
    zl, core = spot // CORES, spot % CORES
    zh = chan // X
    x = chan % X
    x_next, x_last, x_over = (x + 1) % X, (x + 3) % X, (x + 2) % X
    to_next = {"chan": zh * X + x_next}
    to_last = {"chan": zh * X + x_last}
    to_z = {"chan": (1 - zh) * X + x}
    near_core = [{"slab": slab + 1 - 2 * core}]
    near_z = [{"slab": y * PLANE + (zl + hop) % ZL * CORES + core} for hop in range(1, ZL)]
    near_y = [{"slab": (y + hop) % Y * PLANE + spot} for hop in range(1, Y)]

    coups = (coup_0, coup_1, coup_2, coup_3)
    loads = [
        pltpu.make_async_copy(
            coup_hbm.at[pl.ds(i * SHARE, SHARE)], coups[i].at[pl.ds(0, SHARE)], in_sem.at[i]
        )
        for i in range(LOADS)
    ] + [
        pltpu.make_async_copy(given, held, in_sem.at[LOADS + i])
        for i, (given, held) in enumerate(
            ((iter_hbm, itv), (diag_hbm, diag), (reg_hbm, reg), (irr_hbm, irr), (src_hbm, src))
        )
    ]
    prof_load = pltpu.make_async_copy(prof_hbm, prof, in_sem.at[LOADS + 6])
    first_loads, later_loads = loads[: LOADS + 1], loads[LOADS + 1 :] + [prof_load]
    loads[LOADS].start()
    for load in loads[:LOADS]:
        load.start()

    barrier = pltpu.get_barrier_semaphore()
    for peer in (to_next, to_last, to_z):
        pl.semaphore_signal(barrier, inc=1, device_id=peer, device_id_type=MESH)
    for peer in near_core + near_z + near_y:
        pl.semaphore_signal(barrier, inc=1, device_id=peer, device_id_type=MESH)

    shape = (BLOCKS, 2 * BS)
    found = jnp.full(shape, SHARE, jnp.int32)
    square[:PAIRS, :BLOCKS] = pairs[...]
    named = square[...].T
    for p in range(PAIRS):
        found = jnp.where(named[:BLOCKS, p : p + 1] == iota(shape, 1), iota(shape, 0) % (SHARE // PAIRS) * PAIRS + p, found)
    table_v[...] = found
    to_scalars = pltpu.make_async_copy(table_v, table, in_sem.at[LOADS + 5])
    to_scalars.start()
    for coup in coups:
        coup[SHARE] = jnp.zeros((BS, BS), jnp.bfloat16)

    def aligned(row):
        return pl.multiple_of(row, 64)

    def dest(step, x_of):
        z_of = jnp.where(step < HALF, 1 - zh, zh)
        return (z_of * X + x_of) * CHANNELS

    def lower(step, at, x_of):
        return aligned(dest(step, x_of) + at)

    def upper(step, at, x_of):
        return aligned(dest(step, x_of) + at + HALF_ROWS)

    def landed(step, at):
        return jnp.where(step < HALF, 0, HALF_ROWS) + at

    def remote(src_ref, dst_ref, send, recv, peer):
        return pltpu.make_async_remote_copy(
            src_ref=src_ref, dst_ref=dst_ref, send_sem=send, recv_sem=recv,
            device_id=peer, device_id_type=MESH,
        )

    def x_copy(kind, step, at, rows):
        src_row, peer = (
            (lower(step, at, x_over), to_next),
            (upper(step, at, x_over), to_last),
            (upper(step, at, x_next), to_next),
            (lower(step, at, x_last), to_last),
            (lower(step, at, x_next), to_next),
            (upper(step, at, x_last), to_last),
        )[kind]
        if kind < 2:
            landing, first = relayed, 2 * landed(step, at) + kind * rows
        else:
            landing, first = arrived, 4 * landed(step, at) + (kind - 2) * rows
        return remote(
            part.at[pl.ds(src_row, rows)], landing.at[pl.ds(aligned(first), rows)],
            x_send.at[kind], x_recv.at[0 if kind < 2 else 1, step], peer,
        )

    def x_start(kinds, step, at, rows):
        for kind in kinds:
            x_copy(kind, step, at, rows).start()

    def x_wait(place, step, at, rows):
        landing, count = ((relayed, 2), (arrived, 4))[place]
        whole = landing.at[pl.ds(aligned(count * landed(step, at)), count * rows)]
        remote(whole, whole, x_send.at[0], x_recv.at[place, step], to_next).wait_recv()

    def z_copy(step):
        rows = pl.ds(aligned(step * 2 * PIECE), 2 * PIECE)
        return remote(z_out.at[rows], z_in.at[rows], z_send.at[0], z_recv.at[step], to_z)

    levels = (
        (CORES, core, own_0, near_0, near_core),
        (ZL, zl, own_1, near_1, near_z),
        (Y, y, own_2, near_2, near_y),
    )

    def spans(at, rows):
        return pl.ds(at * 2 // BS, rows * 2 // BS)

    def scan_start(level, slot, at, rows):
        _, _, own, near, peers = levels[level]
        here = spans(at, rows)
        for i, peer in enumerate(peers):
            remote(
                own.at[here], near.at[i, here], scan_send.at[level], scan_recv.at[level, slot], peer
            ).start()

    def scan_wait(level, slot, at, rows):
        _, _, _, near, peers = levels[level]
        whole = near.at[:, spans(at, rows)]
        remote(whole, whole, scan_send.at[level], scan_recv.at[level, slot], peers[0]).wait_recv()

    def scan_total(level, here):
        size, _, own, near, _ = levels[level]
        return sum((near[i, here] for i in range(size - 1)), own[here])

    def scan_part(level, here, lanes, later):
        size, mine, _, near, _ = levels[level]
        terms = []
        for i in range(size - 1):
            whose = (mine + size - 1 - i) % size
            counts = whose > mine if later else whose < mine
            terms.append(jnp.where(counts, near[i, here, lanes, :], 0.0))
        return sum(terms[1:], terms[0])

    def out_copy(at, rows, half):
        here = pl.ds(aligned(at + half * HALF_ROWS), rows)
        return pltpu.make_async_copy(out.at[here], out_hbm.at[here], out_sem.at[0])

    def place(step):
        return lax.rem(step, HALF) * PIECE

    def multiply(step, group, ready=None):
        x_a = (x + jnp.where(group == 0, 2, jnp.where(group == 3, 0, 1))) % X
        x_b = (x + jnp.where(group == 0, 2, jnp.where(group == 3, 0, 3))) % X
        cross = group == 1
        at = place(step)
        row_a = aligned(dest(step, x_a) + at + jnp.where(cross, HALF_ROWS, 0))
        row_b = aligned(dest(step, x_b) + at + jnp.where(cross, 0, HALF_ROWS))
        block_a, block_b = row_a // BS, row_b // BS
        blocks = (block_a, block_a + 1, block_b, block_b + 1)
        total = jnp.zeros((2 * PIECE, BS), F32)
        for pair in range(BLOCKS // 2):
            if ready is not None:
                ready(pair)
            coup = coups[2 * pair * PAIRS // SHARE]
            left = jnp.concatenate(
                [
                    jnp.concatenate([coup[table[2 * pair + k, block]] for k in range(2)], axis=1)
                    for block in blocks
                ],
                axis=0,
            )
            right = itv[pl.ds(pair * 2 * BS, 2 * BS), :]
            total = total + jnp.dot(left, right, preferred_element_type=F32)
        part[pl.ds(row_a, PIECE)] = total[:PIECE]
        part[pl.ds(row_b, PIECE)] = total[PIECE:]

    spread = (iota((POINTS, BS), 1) // SIDES == iota((POINTS, BS), 0)).astype(F32)
    sides = (iota((SIDES, BS), 1) % SIDES == iota((SIDES, BS), 0)).astype(F32)
    from_n, to_n = iota((BS, BS), 0), iota((BS, BS), 1)
    same_side = from_n % SIDES == to_n % SIDES
    upto = (same_side & (from_n // SIDES <= to_n // SIDES)).astype(F32)
    above = (same_side & (from_n // SIDES > to_n // SIDES)).astype(F32)

    def profile_row():
        return jnp.dot(prof[...], spread, precision=HIGH, preferred_element_type=F32)

    quad_step = 1.0 / math.sqrt(POINTS * Y * PLANE)

    def both(ref, at, rows):
        return jnp.concatenate(
            [ref[pl.ds(aligned(at), rows), :], ref[pl.ds(aligned(at + HALF_ROWS), rows), :]], axis=0
        )

    def expand(step):
        for half in range(2):
            here = pl.ds(pl.multiple_of(step * PIECE + half * HALF_ROWS, PIECE), PIECE)
            reg_e[here] = dot0(reg[:, here], spread)
            irr_e[here] = dot0(irr[:, here], spread)
            drv0[here] = dot0(diag[:, here], spread) * itv[here, :].astype(F32)

    def combine(step, at, rows):
        x_wait(0, step, at, rows)
        lo, hi = pl.ds(lower(step, at, x_next), rows), pl.ds(upper(step, at, x_last), rows)
        base = 2 * landed(step, at)
        part[lo] = part[lo] + relayed[pl.ds(aligned(base), rows)]
        x_start((4,), step, at, rows)
        part[hi] = part[hi] + relayed[pl.ds(aligned(base + rows), rows)]
        x_start((5,), step, at, rows)

    def own_sums(step, at, rows):
        x_wait(1, step, at, rows)
        base = 4 * landed(step, at)
        up_own, lo_own, lo_sum, up_sum = [
            arrived[pl.ds(aligned(base + i * rows), rows)] for i in range(4)
        ]
        lo = part[pl.ds(lower(step, at, x), rows)] + lo_own + lo_sum
        hi = part[pl.ds(upper(step, at, x), rows)] + up_own + up_sum
        return lo, hi

    def finish_far(step):
        lo, hi = own_sums(step, step * PIECE, PIECE)
        z_out[pl.ds(aligned(step * 2 * PIECE), PIECE)] = lo
        z_out[pl.ds(aligned(step * 2 * PIECE + PIECE), PIECE)] = hi
        z_copy(step).start()

    def finish_near(step, slot, at, rows, crossed):
        if crossed is not None:
            z_copy(crossed).wait_recv()
        lo, hi = own_sums(step, at, rows)
        base = at // PIECE * PIECE + at
        lo = lo + z_in[pl.ds(aligned(base), rows)]
        hi = hi + z_in[pl.ds(aligned(base + PIECE), rows)]
        coupled = jnp.concatenate([lo, hi], axis=0)
        driving = (both(drv0, at, rows) + profile_row() * coupled) * quad_step
        regular, irregular = both(reg_e, at, rows), both(irr_e, at, rows)
        outs, ins = regular * driving, irregular * driving
        totals = jnp.concatenate([dot1(sides, outs), dot1(sides, ins)], axis=0)
        for i in range(2 * rows // BS):
            own_0[at * 2 // BS + i] = totals[:, i * BS : (i + 1) * BS]
        scan_start(0, slot, at, rows)
        outward = jnp.dot(outs, upto, precision=HIGH, preferred_element_type=F32)
        inward = jnp.dot(ins, above, precision=HIGH, preferred_element_type=F32)
        result = both(src, at, rows).astype(F32) + irregular * outward + regular * inward
        local[pl.ds(aligned(at), rows)] = result[:rows]
        local[pl.ds(aligned(at + HALF_ROWS), rows)] = result[rows:]

    def chip_sum(slot, at, rows):
        scan_wait(0, slot, at, rows)
        own_1[spans(at, rows)] = scan_total(0, spans(at, rows))
        scan_start(1, slot, at, rows)

    def plane_sum(slot, at, rows):
        scan_wait(1, slot, at, rows)
        own_2[spans(at, rows)] = scan_total(1, spans(at, rows))
        scan_start(2, slot, at, rows)

    def emit(slot, at, rows):
        here = spans(at, rows)
        count = 2 * rows // BS

        sides_of = ((pl.ds(0, SIDES), False), (pl.ds(SIDES, SIDES), True))
        carries = [
            scan_part(0, here, lanes, later) + scan_part(1, here, lanes, later)
            for lanes, later in sides_of
        ]
        scan_wait(2, slot, at, rows)
        outward, inward = [
            jnp.concatenate([total[i] for i in range(count)], axis=1)
            for total in (
                carry + scan_part(2, here, lanes, later)
                for carry, (lanes, later) in zip(carries, sides_of)
            )
        ]
        updated = both(local, at, rows)
        updated = updated + both(irr_e, at, rows) * dot0(outward, sides)
        updated = updated + both(reg_e, at, rows) * dot0(inward, sides)
        updated = updated.astype(jnp.bfloat16)
        for half in range(2):
            out[pl.ds(aligned(at + half * HALF_ROWS), rows), :] = updated[half * rows : (half + 1) * rows]
            out_copy(at, rows, half).start()

    def regular_piece(call, piece):
        call(piece, piece * PIECE, PIECE)

    to_scalars.wait()
    loads[LOADS].wait()

    def ready(pair):
        if pair % (BLOCKS // 2 // LOADS) == 0:
            loads[pair // (BLOCKS // 2 // LOADS)].wait()

    multiply(0, 0, ready)
    for load in later_loads:
        load.start()
    pl.semaphore_wait(barrier, 3 + 1 + (ZL - 1) + (Y - 1))
    x_start((0, 1), 0, 0, PIECE)
    multiply(0, 1)
    x_start((2, 3), 0, 0, PIECE)

    def multiply_more(step, first):
        def one_group(group, _):
            multiply(step, group)
            return 0

        lax.fori_loop(first, 4, one_group, 0)

    multiply_more(0, 2)
    for load in later_loads:
        load.wait()

    def one_step(step, _):
        @pl.when(step >= 1)
        def _():
            at = place(step)
            x_start((0, 1), step, at, PIECE)
            combine(step - 1, place(step - 1), PIECE)
            x_start((2, 3), step, at, PIECE)

        @pl.when((step >= 2) & (step < HALF + 2))
        def _():
            finish_far(step - 2)

        @pl.when(step >= HALF + 2)
        def _():
            piece = step - HALF - 2
            finish_near(step - 2, piece, piece * PIECE, PIECE, piece)

        multiply_more(step + 1, 0)

        @pl.when(step < HALF)
        def _():
            expand(step)

        @pl.when(step >= HALF + 3)
        def _():
            regular_piece(chip_sum, step - HALF - 3)

        @pl.when(step >= HALF + 4)
        def _():
            regular_piece(plane_sum, step - HALF - 4)

        return 0

    lax.fori_loop(0, STEPS - 1, one_step, 0)

    last = STEPS - 1

    def send(kinds, i):
        x_start(kinds, last + i, *TAIL[i])

    def meet(i):
        combine(last + i, *TAIL[i])

    def finish(i):
        finish_near(last + i, HALF - 1 + i, *TAIL[i], HALF - 1 if i == 0 else None)

    def finish_regular(piece):
        finish_near(HALF + piece, piece, piece * PIECE, PIECE, piece)

    def small_piece(call, i):
        call(HALF - 1 + i, *TAIL[i])

    send((0, 1), 0)
    combine(last - 1, (HALF - 2) * PIECE, PIECE)
    send((2, 3), 0)
    send((0, 1), 1)
    send((2, 3), 1)
    send((0, 1), 2)
    finish_regular(3)
    meet(0)
    send((2, 3), 2)
    regular_piece(chip_sum, 2)
    regular_piece(plane_sum, 1)
    regular_piece(emit, 0)
    meet(1)
    meet(2)
    finish_regular(4)
    regular_piece(chip_sum, 3)
    regular_piece(plane_sum, 2)
    finish(0)
    regular_piece(chip_sum, 4)
    small_piece(chip_sum, 0)
    finish(1)
    finish(2)
    regular_piece(plane_sum, 3)
    small_piece(chip_sum, 1)
    small_piece(chip_sum, 2)
    regular_piece(emit, 1)
    regular_piece(plane_sum, 4)
    small_piece(plane_sum, 0)
    small_piece(plane_sum, 1)
    small_piece(plane_sum, 2)
    regular_piece(emit, 2)
    regular_piece(emit, 3)
    regular_piece(emit, 4)
    for i in range(len(TAIL)):
        small_piece(emit, i)

    for kind in range(6):
        whole = part.at[pl.ds(0, CHANNELS)]
        remote(whole, whole, x_send.at[kind], x_recv.at[0, 0], to_next).wait_send()
    remote(z_out, z_in, z_send.at[0], z_recv.at[0], to_z).wait_send()
    for level, (_, _, _, near, peers) in enumerate(levels):
        remote(near, near, scan_send.at[level], scan_recv.at[level, 0], peers[0]).wait_send()
    pltpu.make_async_copy(out, out_hbm, out_sem.at[0]).wait()


def per_device(iterate, source, coupling, pair_rows, diag_pot, profile, regular, irregular):
    anywhere = pl.BlockSpec(memory_space=pl.ANY)
    wide = pltpu.VMEM((CHANNELS, BS), F32)
    whole = pltpu.VMEM((CHANNELS, BS), jnp.bfloat16)
    narrow = pltpu.VMEM((POINTS, CHANNELS), F32)
    def tiles(*count):
        return pltpu.VMEM((*count, CHANNELS // BS, 2 * SIDES, BS), F32)

    share = pltpu.VMEM((SHARE + 1, BS, BS), jnp.bfloat16)
    dma = pltpu.SemaphoreType.DMA
    result = jax.ShapeDtypeStruct((CHANNELS, BS), jnp.bfloat16)
    updated = pl.pallas_call(
        sweep,
        out_shape=result,
        in_specs=[pl.BlockSpec(memory_space=pltpu.VMEM)] + [anywhere] * 7,
        out_specs=anywhere,
        scratch_shapes=[
            pltpu.VMEM((BS, BS), jnp.int32),
            pltpu.VMEM((1, POINTS), F32),
            pltpu.VMEM((BLOCKS, 2 * BS), jnp.int32),
            pltpu.SMEM((BLOCKS, 2 * BS), jnp.int32),
            share, share, share, share,
            whole, whole, narrow, narrow, narrow, whole,
            pltpu.VMEM((ROW_BLOCKS * BS, BS), F32),
            pltpu.VMEM((2 * CHANNELS, BS), F32),
            pltpu.VMEM((4 * CHANNELS, BS), F32),
            wide, wide, wide, wide, wide, wide,
            tiles(), tiles(), tiles(), tiles(CORES - 1), tiles(ZL - 1), tiles(Y - 1),
            dma((LOADS + 7,)), dma((1,)),
            dma((6,)), dma((2, SENDS)),
            dma((1,)), dma((HALF,)),
            dma((3,)), dma((3, HALF - 1 + len(TAIL))),
        ],
        compiler_params=pltpu.CompilerParams(
            collective_id=0, has_side_effects=True, vmem_limit_bytes=60 * 2**20
        ),
        name="sweep",
    )(
        pair_rows.T,
        coupling.reshape(BLOCKS * PAIRS, BS, BS),
        iterate,
        source,
        diag_pot.T,
        profile.reshape(1, POINTS),
        regular.T,
        irregular.T,
    )
    return updated


def solution(mesh):
    placed = (
        P("chan", "slab"),
        P("chan", "slab"),
        P("chan", None, None, None),
        P("chan", None),
        P("chan", "slab"),
        P("slab"),
        P("chan", "slab"),
        P("chan", "slab"),
    )
    return jax.shard_map(
        per_device, mesh=mesh, in_specs=placed, out_specs=P("chan", "slab"), check_vma=False
    )
```

time: 743 us -> 133 us (0.18); the launches traced: 734 us -> 132 us
  waiting for transfers between devices: 438 us -> 0 us
  starting transfers between devices: 134 us -> 0 us
  Pallas kernels: 0 us -> 130 us
  other arithmetic: 109 us -> 0 us
  local copies, waits for them, and re-layouts: 29 us -> 2.06 us
  between operations: 13.5 us -> 0.01 us
  matrix products: 10.4 us -> 0 us
    reduce_scatter x1 -> x0, waiting for transfers between devices: 242 us -> none  [per_device(): lax.psum_scatter(row_sums, 'chan', scatter_dimension=0, tiled=True)]
    ppermute x62 -> x0, waiting for transfers between devices: 195 us -> none  [shifted(): return lax.ppermute(shard, axis, pairs)]
    ppermute x62 -> x0, starting transfers between devices: 134 us -> none  [shifted(): return lax.ppermute(shard, axis, pairs)]
    pallas_call x0 -> x1, Pallas kernels: none -> 130 us  [per_device(): pl.pallas_call(sweep, out_shape=result, in_specs=[pl.BlockSpec(memory_spa...]
    scatter-add x1 -> x0, other arithmetic: 59.8 us -> none  [per_device(): row_sums = jax.ops.segment_sum(products, targets, num_segments=total_blocks)]
    add x62 -> x0, other arithmetic: 40.3 us -> none  [the longest x31 20.2 us: relay_step(): carry_out = shifted(carry_out + outward_total, 'slab', 1)]
    reshape x2 -> x0, local copies, waits for them, and re-layouts: 14.1 us -> none  [the longest x1 12.6 us: per_device(): row_sums = row_sums.reshape(total_blocks * block_size, columns_all)]
    dot_general x1 -> x0, matrix products: 10.4 us -> none  [per_device(): jnp.einsum('jpab,jbr->jpar', coupling, iterate_blocks, preferred_element_...]
  transfers between devices with their start and end apart: 63 -> 0, of which waited for: 32 -> 0; matrix products, arithmetic and copies ran while one was open for 3% -> 0% of each run, Pallas kernels for 0% -> 0%
where the time goes in v2:
time: 133 us; the launch traced here: 132 us
  Pallas kernels  130 us (98%)
  local copies, waits for them, and re-layouts  2.06 us (2%)
    pallas_call x1, Pallas kernels, per_device(): pl.pallas_call(sweep, out_shape=result, in_specs=[pl.BlockSpec(memory_spa...  130 us

profile of v2, /device:TPU:1, one launch (start us, length us, event | category | flops | bytes accessed | tf_op | source)
XLA Modules:
  0.0 132.4 jit_solution(9188142911252455248)
XLA Ops:
  0.0 130.3 %sweep.1 = bf16[3072,128]{1,0:T(8,128)(2,1)} custom-call(s32[12,24]{1,0:T(8,128)} %bitcast.10, bf16[288,128,128]{2,1,0:T(8,128)(2,1)} %bitcast.6, bf16[3072,128]{1,0:T(8,128)(2,1)} %iter_hbm.1, bf16[3072,128]{1,0:T(8,128)(2,1)} %src_hbm.1, f32[16,3072]{1,0:T(8,128)} %bitcast.7, f32[1,16]{1,0:T(1,128)} %bitcast.11, f32[16,3072]{1,0:T(8,128)} %bitcast.8, ...), custom_call_target="tpu_custom_call" | custom-call | tf_op jit(solution)/shard_map/sweep/pallas_call | solution.py:466
  130.4 2.1 %copy.10 = bf16[3072,128]{1,0:T(8,128)(2,1)} copy(bf16[3072,128]{1,0:T(8,128)(2,1)} %sweep.1) | data formatting | bytes 1572864

commit v3 on v2

--- a/solution.py
+++ b/solution.py
@@ -341,29 +341,40 @@
         load.start()
     pl.semaphore_wait(barrier, 3 + 1 + (ZL - 1) + (Y - 1))
     x_start((0, 1), 0, 0, PIECE)
-    multiply(0, 1)
-    x_start((2, 3), 0, 0, PIECE)
-
-    def multiply_more(step, first):
-        def one_group(group, _):
-            multiply(step, group)
-            return 0
-
-        lax.fori_loop(first, 4, one_group, 0)
-
-    multiply_more(0, 2)
+    def first_groups(i, _):
+        step = jnp.where((i == 0) | (i == 2) | (i == 8), 0, jnp.where(i < 5, 1, 2))
+        group = jnp.where(i < 2, 1 - i, jnp.where(i < 5, i - jnp.where(i == 2, 0, 2), i - 5))
+        multiply(step, group)
+
+        @pl.when(i == 0)
+        def _():
+            x_start((2, 3), 0, 0, PIECE)
+
+        @pl.when(i == 1)
+        def _():
+            x_start((0, 1), 1, PIECE, PIECE)
+
+        @pl.when(i == 2)
+        def _():
+            combine(0, 0, PIECE)
+
+        @pl.when(i == 3)
+        def _():
+            x_start((2, 3), 1, PIECE, PIECE)
+
+        return 0
+
+    lax.fori_loop(0, 9, first_groups, 0)
     for load in later_loads:
         load.wait()
 
     def one_step(step, _):
-        @pl.when(step >= 1)
-        def _():
-            at = place(step)
-            x_start((0, 1), step, at, PIECE)
-            combine(step - 1, place(step - 1), PIECE)
-            x_start((2, 3), step, at, PIECE)
-
-        @pl.when((step >= 2) & (step < HALF + 2))
+        at = place(step)
+        x_start((0, 1), step, at, PIECE)
+        combine(step - 1, place(step - 1), PIECE)
+        x_start((2, 3), step, at, PIECE)
+
+        @pl.when(step < HALF + 2)
         def _():
             finish_far(step - 2)
 
@@ -372,23 +383,31 @@
             piece = step - HALF - 2
             finish_near(step - 2, piece, piece * PIECE, PIECE, piece)
 
-        multiply_more(step + 1, 0)
-
-        @pl.when(step < HALF)
-        def _():
-            expand(step)
-
         @pl.when(step >= HALF + 3)
         def _():
-            regular_piece(chip_sum, step - HALF - 3)
-
-        @pl.when(step >= HALF + 4)
-        def _():
-            regular_piece(plane_sum, step - HALF - 4)
+            regular_piece(plane_sum, step - HALF - 3)
+
+        def one_group(group, _):
+            multiply(jnp.where(group == 3, step - 1, step + 1), group)
+            return 0
+
+        lax.fori_loop(0, 4, one_group, 0)
+
+        @pl.when(step < HALF + 2)
+        def _():
+            expand(step - 2)
+
+        @pl.when(step >= HALF + 2)
+        def _():
+            regular_piece(chip_sum, step - HALF - 2)
+
+        @pl.when(step >= HALF + 3)
+        def _():
+            regular_piece(emit, step - HALF - 3)
 
         return 0
 
-    lax.fori_loop(0, STEPS - 1, one_step, 0)
+    lax.fori_loop(2, STEPS - 1, one_step, 0)
 
     last = STEPS - 1
 
@@ -414,31 +433,33 @@
     send((2, 3), 1)
     send((0, 1), 2)
     finish_regular(3)
+    regular_piece(plane_sum, 2)
     meet(0)
     send((2, 3), 2)
-    regular_piece(chip_sum, 2)
-    regular_piece(plane_sum, 1)
-    regular_piece(emit, 0)
+    regular_piece(chip_sum, 3)
+
+    def own_group(step, _):
+        multiply(step, 3)
+        return 0
+
+    lax.fori_loop(last - 1, last + 1, own_group, 0)
     meet(1)
     meet(2)
+    regular_piece(emit, 2)
     finish_regular(4)
-    regular_piece(chip_sum, 3)
-    regular_piece(plane_sum, 2)
+    regular_piece(plane_sum, 3)
     finish(0)
     regular_piece(chip_sum, 4)
     small_piece(chip_sum, 0)
     finish(1)
     finish(2)
-    regular_piece(plane_sum, 3)
     small_piece(chip_sum, 1)
     small_piece(chip_sum, 2)
-    regular_piece(emit, 1)
+    regular_piece(emit, 3)
     regular_piece(plane_sum, 4)
     small_piece(plane_sum, 0)
     small_piece(plane_sum, 1)
     small_piece(plane_sum, 2)
-    regular_piece(emit, 2)
-    regular_piece(emit, 3)
     regular_piece(emit, 4)
     for i in range(len(TAIL)):
         small_piece(emit, i)

time: 133 us -> 138 us (1.038)
  Pallas kernels: 130 us -> 135 us
    pallas_call x1, Pallas kernels: 130 us -> 135 us  [per_device(): pl.pallas_call(sweep, out_shape=result, in_specs=[pl.BlockSpec(memory_spa...]
where the time goes in v3:
time: 138 us; the launch traced here: 137 us
  Pallas kernels  135 us (98%)
  local copies, waits for them, and re-layouts  2.06 us (1%)
    pallas_call x1, Pallas kernels, per_device(): pl.pallas_call(sweep, out_shape=result, in_specs=[pl.BlockSpec(memory_spa...  135 us

profile of v3, /device:TPU:1, one launch (start us, length us, event | category | flops | bytes accessed | tf_op | source)
XLA Modules:
  0.0 137.4 jit_solution(12390802902747097078)
XLA Ops:
  0.0 135.4 %sweep.1 = bf16[3072,128]{1,0:T(8,128)(2,1)} custom-call(s32[12,24]{1,0:T(8,128)} %bitcast.10, bf16[288,128,128]{2,1,0:T(8,128)(2,1)} %bitcast.6, bf16[3072,128]{1,0:T(8,128)(2,1)} %iter_hbm.1, bf16[3072,128]{1,0:T(8,128)(2,1)} %src_hbm.1, f32[16,3072]{1,0:T(8,128)} %bitcast.7, f32[1,16]{1,0:T(1,128)} %bitcast.11, f32[16,3072]{1,0:T(8,128)} %bitcast.8, ...), custom_call_target="tpu_custom_call" | custom-call | tf_op jit(solution)/shard_map/sweep/pallas_call | solution.py:487
  135.4 2.1 %copy.10 = bf16[3072,128]{1,0:T(8,128)(2,1)} copy(bf16[3072,128]{1,0:T(8,128)(2,1)} %sweep.1) | data formatting | bytes 1572864

commit v4 on v3

--- a/solution.py
+++ b/solution.py
@@ -20,6 +20,7 @@
 STEPS = 12
 HALF = 6
 PIECE = 256
+MIX = 1
 TAIL = ((1280, 128), (1408, 64), (1472, 64))
 SENDS = STEPS - 1 + len(TAIL)
 LOADS = 4
@@ -44,9 +45,9 @@
 def sweep(
     pairs, coup_hbm, iter_hbm, src_hbm, diag_hbm, prof_hbm, reg_hbm, irr_hbm, out_hbm,
     square, prof, table_v, table, coup_0, coup_1, coup_2, coup_3, itv, src, diag, reg, irr, out,
-    part, relayed, arrived, z_out, z_in,
+    part, relayed, arrived, z_out, z_in, crossed,
     drv0, reg_e, irr_e, local, own_0, own_1, own_2, near_0, near_1, near_2,
-    in_sem, out_sem, x_send, x_recv, z_send, z_recv,
+    in_sem, out_sem, x_send, x_recv, z_send, z_recv, cross_send, cross_recv,
     scan_send, scan_recv,
 ):
     slab = lax.axis_index("slab")
@@ -152,6 +153,14 @@
     def z_copy(step):
         rows = pl.ds(aligned(step * 2 * PIECE), 2 * PIECE)
         return remote(z_out.at[rows], z_in.at[rows], z_send.at[0], z_recv.at[step], to_z)
+
+    def cross_copy(side, step):
+        src_row = (lower(step, step * PIECE, x_next), upper(step, step * PIECE, x_last))[side]
+        return remote(
+            part.at[pl.ds(src_row, PIECE)],
+            crossed.at[pl.ds(aligned((2 * step + side) * PIECE), PIECE)],
+            cross_send.at[0], cross_recv.at[step], to_z,
+        )
 
     levels = (
         (CORES, core, own_0, near_0, near_core),
@@ -250,24 +259,55 @@
         lo, hi = pl.ds(lower(step, at, x_next), rows), pl.ds(upper(step, at, x_last), rows)
         base = 2 * landed(step, at)
         part[lo] = part[lo] + relayed[pl.ds(aligned(base), rows)]
-        x_start((4,), step, at, rows)
         part[hi] = part[hi] + relayed[pl.ds(aligned(base + rows), rows)]
-        x_start((5,), step, at, rows)
-
-    def own_sums(step, at, rows):
-        x_wait(1, step, at, rows)
+        if rows < PIECE:
+            x_start((4, 5), step, at, rows)
+            return
+        step = jnp.int32(step)
+
+        @pl.when(step < MIX)
+        def _():
+            cross_copy(0, step).start()
+            cross_copy(1, step).start()
+
+        @pl.when((step >= HALF) & (step < HALF + MIX))
+        def _():
+            first = 2 * (step - HALF) * PIECE
+            whole = crossed.at[pl.ds(aligned(first), 2 * PIECE)]
+            remote(whole, whole, cross_send.at[0], cross_recv.at[step - HALF], to_z).wait_recv()
+            part[lo] = part[lo] + crossed[pl.ds(aligned(first), PIECE)]
+            part[hi] = part[hi] + crossed[pl.ds(aligned(first + PIECE), PIECE)]
+
+        @pl.when(step >= MIX)
+        def _():
+            x_start((4, 5), step, at, rows)
+
+    def own_sums(step, at, rows, summed=True):
+        count = 4 if summed else 2
         base = 4 * landed(step, at)
-        up_own, lo_own, lo_sum, up_sum = [
-            arrived[pl.ds(aligned(base + i * rows), rows)] for i in range(4)
-        ]
-        lo = part[pl.ds(lower(step, at, x), rows)] + lo_own + lo_sum
-        hi = part[pl.ds(upper(step, at, x), rows)] + up_own + up_sum
+        whole = arrived.at[pl.ds(aligned(base), count * rows)]
+        remote(whole, whole, x_send.at[0], x_recv.at[1, step], to_next).wait_recv()
+        come = [arrived[pl.ds(aligned(base + i * rows), rows)] for i in range(count)]
+        lo = part[pl.ds(lower(step, at, x), rows)] + come[1]
+        hi = part[pl.ds(upper(step, at, x), rows)] + come[0]
+        if summed:
+            lo, hi = lo + come[2], hi + come[3]
         return lo, hi
 
     def finish_far(step):
-        lo, hi = own_sums(step, step * PIECE, PIECE)
-        z_out[pl.ds(aligned(step * 2 * PIECE), PIECE)] = lo
-        z_out[pl.ds(aligned(step * 2 * PIECE + PIECE), PIECE)] = hi
+        def put(summed):
+            lo, hi = own_sums(step, step * PIECE, PIECE, summed)
+            z_out[pl.ds(aligned(step * 2 * PIECE), PIECE)] = lo
+            z_out[pl.ds(aligned(step * 2 * PIECE + PIECE), PIECE)] = hi
+
+        @pl.when(step < MIX)
+        def _():
+            put(False)
+
+        @pl.when(step >= MIX)
+        def _():
+            put(True)
+
         z_copy(step).start()
 
     def finish_near(step, slot, at, rows, crossed):
@@ -383,10 +423,6 @@
             piece = step - HALF - 2
             finish_near(step - 2, piece, piece * PIECE, PIECE, piece)
 
-        @pl.when(step >= HALF + 3)
-        def _():
-            regular_piece(plane_sum, step - HALF - 3)
-
         def one_group(group, _):
             multiply(jnp.where(group == 3, step - 1, step + 1), group)
             return 0
@@ -397,13 +433,9 @@
         def _():
             expand(step - 2)
 
-        @pl.when(step >= HALF + 2)
-        def _():
-            regular_piece(chip_sum, step - HALF - 2)
-
         @pl.when(step >= HALF + 3)
         def _():
-            regular_piece(emit, step - HALF - 3)
+            regular_piece(chip_sum, step - HALF - 3)
 
         return 0
 
@@ -433,10 +465,9 @@
     send((2, 3), 1)
     send((0, 1), 2)
     finish_regular(3)
-    regular_piece(plane_sum, 2)
     meet(0)
     send((2, 3), 2)
-    regular_piece(chip_sum, 3)
+    regular_piece(chip_sum, 2)
 
     def own_group(step, _):
         multiply(step, 3)
@@ -445,28 +476,35 @@
     lax.fori_loop(last - 1, last + 1, own_group, 0)
     meet(1)
     meet(2)
-    regular_piece(emit, 2)
+    regular_piece(plane_sum, 0)
+    regular_piece(chip_sum, 3)
     finish_regular(4)
-    regular_piece(plane_sum, 3)
+    regular_piece(plane_sum, 1)
     finish(0)
     regular_piece(chip_sum, 4)
     small_piece(chip_sum, 0)
     finish(1)
     finish(2)
     small_piece(chip_sum, 1)
+    regular_piece(plane_sum, 2)
+    regular_piece(plane_sum, 3)
     small_piece(chip_sum, 2)
-    regular_piece(emit, 3)
+    regular_piece(emit, 0)
+    regular_piece(emit, 1)
     regular_piece(plane_sum, 4)
     small_piece(plane_sum, 0)
     small_piece(plane_sum, 1)
     small_piece(plane_sum, 2)
+    regular_piece(emit, 2)
+    regular_piece(emit, 3)
     regular_piece(emit, 4)
     for i in range(len(TAIL)):
         small_piece(emit, i)
 
     for kind in range(6):
-        whole = part.at[pl.ds(0, CHANNELS)]
+        whole = part.at[pl.ds(0, CHANNELS - (MIX * PIECE if kind > 3 else 0))]
         remote(whole, whole, x_send.at[kind], x_recv.at[0, 0], to_next).wait_send()
+    remote(crossed, crossed, cross_send.at[0], cross_recv.at[0], to_z).wait_send()
     remote(z_out, z_in, z_send.at[0], z_recv.at[0], to_z).wait_send()
     for level, (_, _, _, near, peers) in enumerate(levels):
         remote(near, near, scan_send.at[level], scan_recv.at[level, 0], peers[0]).wait_send()
@@ -499,11 +537,11 @@
             pltpu.VMEM((ROW_BLOCKS * BS, BS), F32),
             pltpu.VMEM((2 * CHANNELS, BS), F32),
             pltpu.VMEM((4 * CHANNELS, BS), F32),
-            wide, wide, wide, wide, wide, wide,
+            wide, wide, pltpu.VMEM((2 * MIX * PIECE, BS), F32), wide, wide, wide, wide,
             tiles(), tiles(), tiles(), tiles(CORES - 1), tiles(ZL - 1), tiles(Y - 1),
             dma((LOADS + 7,)), dma((1,)),
             dma((6,)), dma((2, SENDS)),
-            dma((1,)), dma((HALF,)),
+            dma((1,)), dma((HALF,)), dma((1,)), dma((MIX,)),
             dma((3,)), dma((3, HALF - 1 + len(TAIL))),
         ],
         compiler_params=pltpu.CompilerParams(

time: 138 us -> 126 us (0.913)
  Pallas kernels: 135 us -> 124 us
    pallas_call x1, Pallas kernels: 135 us -> 124 us  [per_device(): pl.pallas_call(sweep, out_shape=result, in_specs=[pl.BlockSpec(memory_spa...]
where the time goes in v4:
time: 126 us
  Pallas kernels  124 us (98%)
  local copies, waits for them, and re-layouts  2.06 us (2%)
    pallas_call x1, Pallas kernels, per_device(): pl.pallas_call(sweep, out_shape=result, in_specs=[pl.BlockSpec(memory_spa...  124 us

profile of v4, /device:TPU:1, one launch (start us, length us, event | category | flops | bytes accessed | tf_op | source)
XLA Modules:
  0.0 125.8 jit_solution(17572013005563284973)
XLA Ops:
  0.0 123.7 %sweep.1 = bf16[3072,128]{1,0:T(8,128)(2,1)} custom-call(s32[12,24]{1,0:T(8,128)} %bitcast.10, bf16[288,128,128]{2,1,0:T(8,128)(2,1)} %bitcast.6, bf16[3072,128]{1,0:T(8,128)(2,1)} %iter_hbm.1, bf16[3072,128]{1,0:T(8,128)(2,1)} %src_hbm.1, f32[16,3072]{1,0:T(8,128)} %bitcast.7, f32[1,16]{1,0:T(1,128)} %bitcast.11, f32[16,3072]{1,0:T(8,128)} %bitcast.8, ...), custom_call_target="tpu_custom_call" | custom-call | tf_op jit(solution)/shard_map/sweep/pallas_call | solution.py:525
  123.7 2.1 %copy.10 = bf16[3072,128]{1,0:T(8,128)(2,1)} copy(bf16[3072,128]{1,0:T(8,128)(2,1)} %sweep.1) | data formatting | bytes 1572864

commit v5 on v4

--- a/solution.py
+++ b/solution.py
@@ -21,7 +21,7 @@
 HALF = 6
 PIECE = 256
 MIX = 1
-TAIL = ((1280, 128), (1408, 64), (1472, 64))
+TAIL = ((1280, 128), (1408, 128))
 SENDS = STEPS - 1 + len(TAIL)
 LOADS = 4
 SHARE = BLOCKS * PAIRS // LOADS
@@ -43,8 +43,8 @@
 
 
 def sweep(
-    pairs, coup_hbm, iter_hbm, src_hbm, diag_hbm, prof_hbm, reg_hbm, irr_hbm, out_hbm,
-    square, prof, table_v, table, coup_0, coup_1, coup_2, coup_3, itv, src, diag, reg, irr, out,
+    pairs_hbm, coup_hbm, iter_hbm, src_hbm, diag_hbm, prof_hbm, reg_hbm, irr_hbm, out_hbm,
+    pairs, square, prof, table_v, table, coup_0, coup_1, coup_2, coup_3, itv, src, diag, reg, irr, out,
     part, relayed, arrived, z_out, z_in, crossed,
     drv0, reg_e, irr_e, local, own_0, own_1, own_2, near_0, near_1, near_2,
     in_sem, out_sem, x_send, x_recv, z_send, z_recv, cross_send, cross_recv,
@@ -78,6 +78,8 @@
         )
     ]
     prof_load = pltpu.make_async_copy(prof_hbm, prof, in_sem.at[LOADS + 6])
+    pairs_load = pltpu.make_async_copy(pairs_hbm, pairs, in_sem.at[LOADS + 7])
+    pairs_load.start()
     first_loads, later_loads = loads[: LOADS + 1], loads[LOADS + 1 :] + [prof_load]
     loads[LOADS].start()
     for load in loads[:LOADS]:
@@ -91,6 +93,7 @@
 
     shape = (BLOCKS, 2 * BS)
     found = jnp.full(shape, SHARE, jnp.int32)
+    pairs_load.wait()
     square[:PAIRS, :BLOCKS] = pairs[...]
     named = square[...].T
     for p in range(PAIRS):
@@ -411,8 +414,8 @@
     def one_step(step, _):
         at = place(step)
         x_start((0, 1), step, at, PIECE)
+        x_start((2, 3), step, at, PIECE)
         combine(step - 1, place(step - 1), PIECE)
-        x_start((2, 3), step, at, PIECE)
 
         @pl.when(step < HALF + 2)
         def _():
@@ -458,15 +461,13 @@
     def small_piece(call, i):
         call(HALF - 1 + i, *TAIL[i])
 
-    send((0, 1), 0)
+    for i in range(len(TAIL)):
+        send((0, 1), i)
     combine(last - 1, (HALF - 2) * PIECE, PIECE)
-    send((2, 3), 0)
-    send((0, 1), 1)
-    send((2, 3), 1)
-    send((0, 1), 2)
+    for i in range(len(TAIL)):
+        send((2, 3), i)
     finish_regular(3)
     meet(0)
-    send((2, 3), 2)
     regular_piece(chip_sum, 2)
 
     def own_group(step, _):
@@ -475,26 +476,22 @@
 
     lax.fori_loop(last - 1, last + 1, own_group, 0)
     meet(1)
-    meet(2)
+    regular_piece(chip_sum, 3)
     regular_piece(plane_sum, 0)
-    regular_piece(chip_sum, 3)
     finish_regular(4)
     regular_piece(plane_sum, 1)
+    regular_piece(emit, 0)
     finish(0)
     regular_piece(chip_sum, 4)
     small_piece(chip_sum, 0)
     finish(1)
-    finish(2)
     small_piece(chip_sum, 1)
     regular_piece(plane_sum, 2)
     regular_piece(plane_sum, 3)
-    small_piece(chip_sum, 2)
-    regular_piece(emit, 0)
     regular_piece(emit, 1)
     regular_piece(plane_sum, 4)
-    small_piece(plane_sum, 0)
-    small_piece(plane_sum, 1)
-    small_piece(plane_sum, 2)
+    for i in range(len(TAIL)):
+        small_piece(plane_sum, i)
     regular_piece(emit, 2)
     regular_piece(emit, 3)
     regular_piece(emit, 4)
@@ -525,9 +522,10 @@
     updated = pl.pallas_call(
         sweep,
         out_shape=result,
-        in_specs=[pl.BlockSpec(memory_space=pltpu.VMEM)] + [anywhere] * 7,
+        in_specs=[anywhere] * 8,
         out_specs=anywhere,
         scratch_shapes=[
+            pltpu.VMEM((PAIRS, BLOCKS), jnp.int32),
             pltpu.VMEM((BS, BS), jnp.int32),
             pltpu.VMEM((1, POINTS), F32),
             pltpu.VMEM((BLOCKS, 2 * BS), jnp.int32),
@@ -539,7 +537,7 @@
             pltpu.VMEM((4 * CHANNELS, BS), F32),
             wide, wide, pltpu.VMEM((2 * MIX * PIECE, BS), F32), wide, wide, wide, wide,
             tiles(), tiles(), tiles(), tiles(CORES - 1), tiles(ZL - 1), tiles(Y - 1),
-            dma((LOADS + 7,)), dma((1,)),
+            dma((LOADS + 8,)), dma((1,)),
             dma((6,)), dma((2, SENDS)),
             dma((1,)), dma((HALF,)), dma((1,)), dma((MIX,)),
             dma((3,)), dma((3, HALF - 1 + len(TAIL))),

time: 126 us -> 124 us (0.984)
  Pallas kernels: 124 us -> 122 us
    pallas_call x1, Pallas kernels: 124 us -> 122 us  [per_device(): pl.pallas_call(sweep, out_shape=result, in_specs=[anywhere] * 8, out_spec...]
where the time goes in v5:
time: 124 us
  Pallas kernels  122 us (98%)
  local copies, waits for them, and re-layouts  2.06 us (2%)
    pallas_call x1, Pallas kernels, per_device(): pl.pallas_call(sweep, out_shape=result, in_specs=[anywhere] * 8, out_spec...  122 us

profile of v5, /device:TPU:1, one launch (start us, length us, event | category | flops | bytes accessed | tf_op | source)
XLA Modules:
  0.0 124.2 jit_solution(16363829908952754554)
XLA Ops:
  0.0 122.1 %sweep.1 = bf16[3072,128]{1,0:T(8,128)(2,1)} custom-call(s32[12,24]{1,0:T(8,128)} %bitcast.10, bf16[288,128,128]{2,1,0:T(8,128)(2,1)} %bitcast.6, bf16[3072,128]{1,0:T(8,128)(2,1)} %iter_hbm.1, bf16[3072,128]{1,0:T(8,128)(2,1)} %src_hbm.1, f32[16,3072]{1,0:T(8,128)} %bitcast.7, f32[1,16]{1,0:T(1,128)} %bitcast.11, f32[16,3072]{1,0:T(8,128)} %bitcast.8, ...), custom_call_target="tpu_custom_call" | custom-call | tf_op jit(solution)/shard_map/sweep/pallas_call | solution.py:522
  122.1 2.1 %copy.10 = bf16[3072,128]{1,0:T(8,128)(2,1)} copy(bf16[3072,128]{1,0:T(8,128)(2,1)} %sweep.1) | data formatting | bytes 1572864
